TPU v7x, 32 devices: a whole 2x2x4 slice. The times are simulated.
32 devices in a mesh: ctx: 8 (over y, x, core), tp: 4 (over z).
Axes of the slice: x: 2, y: 2, z: 4, core: 2. Of those that a mesh axis runs over, the one named last changes fastest.
Arguments:
- upstream: bfloat16 [8192, 4096], P('ctx', 'tp'), may hold values from -0.75 to 0.75
- out_weight: bfloat16 [4096, 4096], P('tp'), may hold values from -0.125 to 0.125
- inner_act: bfloat16 [8192, 4096], P('ctx', 'tp'), may hold values from -6 to 6
- head_bc: bfloat16 [8192, 4096], P('ctx', 'tp'), may hold values from -0.75 to 0.75
- log_decay: float32 [32, 8192], P('tp', 'ctx'), may hold values from -1 to 0, as said below
- states: float32 [32, 32, 64, 128], P('ctx', 'tp'), may hold values from -3 to 3
- skip: float32 [32], P('tp'), may hold values from 0.1 to 1.9
Outputs:
- grad_inner: bfloat16 [8192, 4096], P('ctx', 'tp')
- grad_bc: float32 [8192, 4096], P('ctx', 'tp')
- grad_log: float32 [32, 8192], P('tp', 'ctx')
Inputs may be any that keep to these rules, and one draw needn't show every extreme that they name: `log_decay`: every entry is negative.
All inputs are finite; a program needn't handle non-finite values.
Results may differ from a plain program's by a relative error of at most 0.0049.
Values may be sent and summed in bfloat16 or wider, within the bound.
A program may use at most 128 MiB of HBM per device.

v0:
```python
import functools

import jax
import jax.numpy as jnp
from jax import lax
from jax.experimental import pallas as pl
from jax.experimental.pallas import tpu as pltpu
from jax.sharding import PartitionSpec as P

HEAD_DIM = 128
STATE = 64
BLOCK = 256
F32 = jnp.float32
BF16 = jnp.bfloat16
ROWS = (((0,), (0,)), ((), ()))
LANES = (((1,), (1,)), ((), ()))


def cumulative(log_rows):
    earlier = lax.broadcasted_iota(jnp.int32, (BLOCK, BLOCK), 0)
    later = lax.broadcasted_iota(jnp.int32, (BLOCK, BLOCK), 1)
    upto = jnp.where(earlier <= later, 1.0, 0.0)
    rows = jnp.dot(log_rows, upto, precision=lax.Precision.HIGHEST, preferred_element_type=F32)
    return rows, rows.T


def later_terms(c_rows, dy, head_decay):
    weighted = (c_rows.astype(F32) * head_decay).astype(BF16)
    return lax.dot_general(weighted, dy, ROWS, preferred_element_type=F32)


def terms_kernel(heads, bc_ref, dy_ref, log_ref, out_ref):
    @pl.when(pl.program_id(0) == 0)
    def _():
        out_ref[...] = jnp.zeros_like(out_ref)

    rows, cols = cumulative(log_ref[...])
    decay = jnp.exp(cols)
    for h in range(heads):
        c_rows = bc_ref[:, h * 128 + STATE : (h + 1) * 128]
        dy = dy_ref[:, h * 128 : (h + 1) * 128]
        term = later_terms(c_rows, dy, decay[:, h : h + 1])
        out_ref[h] = decay[BLOCK - 1 : BLOCK, h : h + 1] * out_ref[h] + term


def block_kernel(
    heads, x_ref, bc_ref, dy_ref, log_ref, s_ref, skip_ref, in_ref, gx_ref, gbc_ref, glog_ref, h_ref
):
    @pl.when(pl.program_id(0) == 0)
    def _():
        h_ref[...] = in_ref[...]

    rows, cols = cumulative(log_ref[...])
    decay = jnp.exp(cols)
    tail = jnp.exp(cols[BLOCK - 1 : BLOCK, :] - cols)
    k_ids = lax.broadcasted_iota(jnp.int32, (BLOCK, BLOCK), 0)
    q_ids = lax.broadcasted_iota(jnp.int32, (BLOCK, BLOCK), 1)
    causal = q_ids >= k_ids
    sign = jnp.where(lax.broadcasted_iota(jnp.int32, (1, 128), 1) < STATE, -1.0, 1.0)
    lane = lax.broadcasted_iota(jnp.int32, (BLOCK, heads), 1)
    token = lax.broadcasted_iota(jnp.int32, (BLOCK, 1), 0)
    dcum = jnp.zeros((BLOCK, heads), F32)
    for h in range(heads):
        here = slice(h * 128, (h + 1) * 128)
        bc = bc_ref[:, here]
        b_rows, c_rows = bc[:, :STATE], bc[:, STATE:]
        x, dy = x_ref[:, here], dy_ref[:, here]
        carried, start = h_ref[h], s_ref[0, h]
        held, start_low = carried.astype(BF16), start.astype(BF16)
        gap = rows[h : h + 1, :] - cols[:, h : h + 1]
        gate = jnp.exp(jnp.where(causal, gap, -1e30))
        scores = lax.dot_general(b_rows, c_rows, LANES, preferred_element_type=F32) * gate
        inner = lax.dot_general(x, dy, LANES, preferred_element_type=F32) * gate
        scores, inner = scores.astype(BF16), inner.astype(BF16)
        tail_h, decay_h = tail[:, h : h + 1], decay[:, h : h + 1]
        gx = jnp.dot(scores, dy, preferred_element_type=F32)
        gx += tail_h * jnp.dot(b_rows, held, preferred_element_type=F32)
        gx += skip_ref[h] * dy.astype(F32)
        gx_ref[:, here] = gx.astype(BF16)
        gb_tail = tail_h * lax.dot_general(x, held, LANES, preferred_element_type=F32)
        gb = jnp.dot(inner, c_rows, preferred_element_type=F32) + gb_tail
        gc = lax.dot_general(inner, b_rows, ROWS, preferred_element_type=F32)
        gc += decay_h * lax.dot_general(dy, start_low, LANES, preferred_element_type=F32)
        gbc = jnp.concatenate([gb, gc], axis=1)
        gbc_ref[:, here] = gbc
        dcum_h = jnp.sum(bc.astype(F32) * gbc * sign, axis=1, keepdims=True)
        whole = decay[BLOCK - 1 : BLOCK, h : h + 1]
        at_end = whole * jnp.sum(start * carried) + jnp.sum(b_rows.astype(F32) * gb_tail)
        dcum_h = dcum_h + jnp.where(token == BLOCK - 1, at_end, 0.0)
        dcum = jnp.where(lane == h, dcum_h, dcum)
        h_ref[h] = whole * carried + later_terms(c_rows, dy, decay_h)
    from_here = jnp.where(k_ids >= q_ids, 1.0, 0.0)
    glog_ref[...] = jnp.dot(
        dcum.T, from_here, precision=lax.Precision.HIGHEST, preferred_element_type=F32
    )


def later_state(part, part_log, axis):
    count, place = lax.axis_size(axis), lax.axis_index(axis)
    parts = lax.all_gather(part, axis)
    logs = lax.all_gather(part_log, axis)
    ids = jnp.arange(count)[:, None]
    between = jnp.where(ids > place, logs, 0.0)
    before = jnp.cumsum(between, axis=0) - between
    weights = jnp.where(ids > place, jnp.exp(before), 0.0)
    return jnp.sum(weights[:, :, None, None] * parts, axis=0)


def per_device(upstream, out_weight, inner_act, head_bc, log_decay, states, skip):
    tokens, heads = inner_act.shape[0], log_decay.shape[0]
    width = heads * HEAD_DIM
    blocks = tokens // BLOCK
    out_grad = lax.dot_general(
        lax.all_gather(upstream, "tp", axis=1, tiled=True),
        out_weight,
        LANES,
        preferred_element_type=F32,
    ).astype(BF16)
    wide = pl.BlockSpec((BLOCK, width), lambda i: (blocks - 1 - i, 0))
    logs = pl.BlockSpec((heads, BLOCK), lambda i: (0, blocks - 1 - i))
    carry = pl.BlockSpec((heads, STATE, HEAD_DIM), lambda i: (0, 0, 0))
    params = pltpu.CompilerParams(
        dimension_semantics=("arbitrary",), vmem_limit_bytes=48 * 1024 * 1024
    )
    part = pl.pallas_call(
        functools.partial(terms_kernel, heads),
        out_shape=jax.ShapeDtypeStruct((heads, STATE, HEAD_DIM), F32),
        grid=(blocks,),
        in_specs=[wide, wide, logs],
        out_specs=carry,
        compiler_params=params,
        name="part_terms",
    )(head_bc, out_grad, log_decay)
    incoming = later_state(part, jnp.sum(log_decay, axis=1), "ctx")
    return pl.pallas_call(
        functools.partial(block_kernel, heads),
        out_shape=(
            jax.ShapeDtypeStruct((tokens, width), BF16),
            jax.ShapeDtypeStruct((tokens, width), F32),
            jax.ShapeDtypeStruct((heads, tokens), F32),
        ),
        grid=(blocks,),
        in_specs=[
            wide,
            wide,
            wide,
            logs,
            pl.BlockSpec((1, heads, STATE, HEAD_DIM), lambda i: (blocks - 1 - i, 0, 0, 0)),
            pl.BlockSpec(memory_space=pltpu.SMEM),
            carry,
        ],
        out_specs=(wide, wide, logs),
        scratch_shapes=[pltpu.VMEM((heads, STATE, HEAD_DIM), F32)],
        compiler_params=params,
        name="block_gradients",
    )(inner_act, head_bc, out_grad, log_decay, states, skip, incoming)


def solution(mesh):
    return jax.shard_map(
        per_device,
        mesh=mesh,
        in_specs=(
            P("ctx", "tp"),
            P("tp", None),
            P("ctx", "tp"),
            P("ctx", "tp"),
            P("tp", "ctx"),
            P("ctx", "tp", None, None),
            P("tp"),
        ),
        out_specs=(P("ctx", "tp"), P("ctx", "tp"), P("tp", "ctx")),
        check_vma=False,
    )
```

profile of v0, /device:TPU:0, one launch (start us, length us, event | category | flops | bytes accessed | tf_op | source)
XLA Modules:
  0.0 242.8 jit_solution(7461987065652702352)
XLA Ops:
  7.2 0.0 all-gather.5.cloned.1.call-start
  7.2 0.7 all-gather.5.cloned.1.call-update
  7.9 0.0 copy-start
  7.9 0.0 copy-start.4
  7.9 0.0 all-gather.7.cloned.1.call-start
  8.0 154.0 %all-gather.5.cloned.1.call-done = bf16[1024,4096]{1,0:T(8,128)(2,1)} async-done(((bf16[1024,1024]{1,0:T(8,128)(2,1)}), bf16[1024,4096]{1,0:T(8,128)(2,1)}) %all-gather.5.cloned.1.call-update) | async-done | bytes 8388624 | tf_op jit(solution)/shard_map/all_gather | solution.py:114
  161.9 13.7 %convolution_convert_fusion.dy_ref = bf16[1024,1024]{1,0:T(8,128)(2,1)S(1)} fusion(bf16[1024,4096]{1,0:T(8,128)(2,1)} %all-gather.5.cloned.1.call-done, bf16[1024,4096]{1,0:T(8,128)(2,1)} %param.8), kind=kOutput, calls=%fused_computation.1 | convolution fusion | flops 8590983168 | bytes 18874368 | tf_op jit(solution)/shard_map/dot_general | solution.py:113
  175.7 0.0 copy-done
  175.7 0.0 copy-done.4
  175.7 0.0 copy-start.6
  175.7 0.0 copy-start.3
  175.7 0.0 copy-start.5
  175.7 6.7 %part_terms.1 = f32[8,64,128]{2,1,0:T(8,128)} custom-call(bf16[1024,1024]{1,0:T(8,128)(2,1)S(1)} %copy-done, bf16[1024,1024]{1,0:T(8,128)(2,1)S(1)} %convolution_convert_fusion.dy_ref, f32[8,1024]{1,0:T(8,128)S(1)} %copy-done.4), custom_call_target="tpu_custom_call" | custom-call | tf_op jit(solution)/shard_map/part_terms/pallas_call | solution.py:125
  182.5 0.0 copy-start.1
  182.5 1.3 copy-done.1
  183.8 0.0 all-gather.7.cloned.1.call-update
  183.8 0.1 reduce_sum.18
  184.0 0.0 copy-done.6
  184.0 0.6 dynamic-slice
  185.2 0.2 dynamic-update-slice
  185.5 13.9 %all-reduce = f32[64]{0:T(128)S(1)} all-reduce(f32[64]{0:T(128)S(1)} %dynamic-update-slice), channel_id=2, replica_groups=mesh['ctx'=8,'tp'=4] {'ctx'}, use_global_device_ids=true, to_apply=%add | all-reduce | flops 64 | bytes 512
  199.4 0.1 reshape.12
  199.5 0.1 broadcast_select_fusion
  199.6 0.1 exponential_select_fusion
  199.6 10.5 %all-gather.7.cloned.1.call-done = f32[64,64,128]{2,1,0:T(8,128)} async-done(((f32[8,64,128]{2,1,0:T(8,128)}), f32[64,64,128]{2,1,0:T(8,128)}) %all-gather.7.cloned.1.call-update) | async-done | bytes 2097168 | tf_op jit(solution)/shard_map/all_gather | solution.py:100
  210.1 1.8 multiply_reduce_fusion.in_ref
  212.0 0.0 copy-done.3
  212.0 0.0 copy-done.5
  212.0 0.0 copy-start.2
  212.0 1.6 copy-done.2
  213.6 22.3 %block_gradients.1 = (bf16[1024,1024]{1,0:T(8,128)(2,1)}, f32[1024,1024]{1,0:T(8,128)}, f32[8,1024]{1,0:T(8,128)}) custom-call(bf16[1024,1024]{1,0:T(8,128)(2,1)S(1)} %copy-done.2, bf16[1024,1024]{1,0:T(8,128)(2,1)S(1)} %copy-done, bf16[1024,1024]{1,0:T(8,128)(2,1)} %copy-done.1, f32[8,1024]{1,0:T(8,128)S(1)} %copy-done.4, f32[4,8,64,128]{3,2,1,0:T(8,128)S(1)} %copy-done.3, ...), custom_call_target="tpu_custom_call" | custom-call | tf_op jit(solution)/shard_map/block_gradients/pallas_call | solution.py:135
  (3 shorter events, 0.0 us)
Async XLA Ops:
  7.2 154.8 %all-gather.5.cloned.1.call-start = ((), (), s32[]{:S(2)}) async-start(), calls=%async_computation | async-start | bytes 10485760 | tf_op jit(solution)/shard_map/all_gather | solution.py:114
  7.9 167.8 %copy-start = (bf16[1024,1024]{1,0:T(8,128)(2,1)S(1)}, bf16[1024,1024]{1,0:T(8,128)(2,1)}, u32[]{:S(2)}) copy-start(bf16[1024,1024]{1,0:T(8,128)(2,1)} %bc_ref.3) | copy-start | bytes 6291460
  7.9 167.8 %copy-start.4 = (f32[8,1024]{1,0:T(8,128)S(1)}, f32[8,1024]{1,0:T(8,128)}, u32[]{:S(2)}) copy-start(f32[8,1024]{1,0:T(8,128)} %log_ref.3) | copy-start | bytes 98308
  7.9 202.2 %all-gather.7.cloned.1.call-start = ((), (), s32[]{:S(2)}) async-start(), calls=%async_computation.1 | async-start | bytes 2359296 | tf_op jit(solution)/shard_map/all_gather | solution.py:100
  175.7 8.3 %copy-start.6 = (u32[32]{0:T(128)S(1)}, u32[32]{0:T(128)}, u32[]{:S(2)}) copy-start(u32[32]{0:T(128)} %constant.14) | copy-start | bytes 388
  175.7 36.3 %copy-start.3 = (f32[4,8,64,128]{3,2,1,0:T(8,128)S(1)}, f32[4,8,64,128]{3,2,1,0:T(8,128)}, u32[]{:S(2)}) copy-start(f32[4,8,64,128]{3,2,1,0:T(8,128)} %s_ref.1) | copy-start | bytes 3145732
  175.7 36.3 %copy-start.5 = (f32[8]{0:T(128)S(1)}, f32[8]{0:T(128)}, u32[]{:S(2)}) copy-start(f32[8]{0:T(128)} %skip_ref.1) | copy-start | bytes 100
  182.5 1.3 copy-start.1
  212.0 1.6 copy-start.2
Sparse Core Ops, SparseCore 0:
  9.6 152.3 all-gather.4
  184.0 26.1 all-gather.6
where the time goes:
time: 243 us
  waiting for transfers between devices  165 us (68%)
  Pallas kernels  29.1 us (12%)
  between operations  14.8 us (6%)
  blocking collectives  13.9 us (6%)
  matrix products  13.7 us (6%)
  local copies, waits for them, and re-layouts  3.86 us (2%)
    all_gather x1, waiting for transfers between devices, per_device(): lax.all_gather(upstream, 'tp', axis=1, tiled=True)  154 us
    pallas_call x1, Pallas kernels, per_device(): pl.pallas_call(functools.partial(block_kernel, heads), out_shape=(jax.Sha...  22.3 us
    unnamed x1, blocking collectives  13.9 us
    dot_general x1, matrix products, per_device(): lax.dot_general(lax.all_gather(upstream, 'tp', axis=1, tiled=True), out_w...  13.7 us
    all_gather x1, waiting for transfers between devices, later_state(): parts = lax.all_gather(part, axis)  10.5 us
    pallas_call x1, Pallas kernels, per_device(): pl.pallas_call(functools.partial(terms_kernel, heads), out_shape=jax.Shap...  6.74 us
  transfers between devices with their start and end apart: 2, of which 2 were waited for; matrix products, arithmetic and copies ran while one was open for 1% of the time, Pallas kernels for 0%

commit v1 on v0

--- a/solution.py
+++ b/solution.py
@@ -10,6 +10,7 @@
 HEAD_DIM = 128
 STATE = 64
 BLOCK = 256
+CHUNK = 128
 F32 = jnp.float32
 BF16 = jnp.bfloat16
 ROWS = (((0,), (0,)), ((), ()))
@@ -29,18 +30,383 @@
     return lax.dot_general(weighted, dy, ROWS, preferred_element_type=F32)
 
 
-def terms_kernel(heads, bc_ref, dy_ref, log_ref, out_ref):
-    @pl.when(pl.program_id(0) == 0)
-    def _():
-        out_ref[...] = jnp.zeros_like(out_ref)
-
-    rows, cols = cumulative(log_ref[...])
-    decay = jnp.exp(cols)
+def part_combined(first, second):
+    first_decay = first[STATE : STATE + 1]
+    terms = first[:STATE] + first_decay * second[:STATE]
+    return jnp.concatenate([terms, first[STATE:] * second[STATE:]], axis=0)
+
+
+def project_kernel(
+    tp,
+    ctx,
+    up_hbm,
+    w_hbm,
+    bc_hbm,
+    log_ref,
+    dy_ref,
+    in_ref,
+    got,
+    w_ref,
+    bc_ref,
+    far_w,
+    acc,
+    sum_out,
+    sum_in,
+    weighted,
+    part,
+    sib_part,
+    message,
+    later,
+    half_in,
+    sib_half,
+    local_sem,
+    own_sem,
+    relay_sem,
+    got_sem,
+    sum_send,
+    sum_recv,
+    piece_sem,
+    peer_sem,
+    pair_sem,
+    far_sem,
+    swap_sem,
+    chip_send,
+    chip_recv,
+):
+    z, me = lax.axis_index("tp"), lax.axis_index("ctx")
+    core, chip = lax.rem(me, 2), lax.div(me, 2)
+    sibling = me + 1 - 2 * core
+    chips = ctx // 2
+    heads = log_ref.shape[0]
+    half = heads // 2
+    tokens, depth = up_hbm.shape
+    width = w_hbm.shape[0]
+    piece = width // ctx
+    count = tokens // CHUNK
+    paired = tp == 4
+    has_left, has_right = z > 0, z < tp - 1
+    inner = jnp.logical_and(has_left, has_right)
+    outer = jnp.logical_not(inner)
+
+    def rows_of(c):
+        return pl.ds(pl.multiple_of(c * CHUNK, CHUNK), CHUNK)
+
+    def remote(src, dst, send, recv, **place):
+        return pltpu.make_async_remote_copy(
+            src_ref=src,
+            dst_ref=dst,
+            send_sem=send,
+            recv_sem=recv,
+            device_id=place,
+            device_id_type=pl.DeviceIdType.MESH,
+        )
+
+    def own_copy(c, side):
+        target = z - 1 if side == 0 else z + 1
+        return remote(
+            up_hbm.at[rows_of(c)], got.at[z, rows_of(c)], own_sem.at[side, c], got_sem.at[z, c], tp=target
+        )
+
+    def relay(s, c, target):
+        place = got.at[s, rows_of(c)]
+        return remote(place, place, relay_sem.at[s, c], got_sem.at[s, c], tp=target)
+
+    def each(n, body):
+        lax.fori_loop(0, n, lambda c, unused: (body(c), unused)[1], 0)
+
+    def term(s, c):
+        columns = pl.ds(pl.multiple_of(s * depth, depth), depth)
+        return lax.dot_general(got[s, rows_of(c)], w_ref[:, columns], LANES, preferred_element_type=F32)
+
+    load_w = pltpu.make_async_copy(w_hbm, w_ref, local_sem.at[0])
+    load_up = pltpu.make_async_copy(up_hbm, got.at[z], local_sem.at[1])
+    load_bc = pltpu.make_async_copy(bc_hbm, bc_ref, local_sem.at[2])
+    load_up.start()
+    load_w.start()
+    load_bc.start()
+
+    barrier = pltpu.get_barrier_semaphore()
+
+    def greet(**place):
+        pl.semaphore_signal(barrier, inc=1, device_id=place, device_id_type=pl.DeviceIdType.MESH)
+
+    pl.when(has_left)(lambda: greet(tp=z - 1))
+    pl.when(has_right)(lambda: greet(tp=z + 1))
+    greet(ctx=sibling)
+    for q in range(chips):
+        pl.when(q != chip)(functools.partial(greet, ctx=2 * q + core))
+    pl.semaphore_wait(barrier, chips + has_left.astype(jnp.int32) + has_right.astype(jnp.int32))
+
+    low = jnp.where(z <= 1, 2, 0)
+
+    def piece_place(j):
+        return far_w.at[pl.ds(pl.multiple_of(j * piece, piece), piece)]
+
+    def piece_down():
+        source = w_hbm.at[
+            pl.ds(pl.multiple_of(me * piece, piece), piece),
+            pl.ds(pl.multiple_of(low * depth, depth), 2 * depth),
+        ]
+        return remote(source, piece_place(me), piece_sem, far_sem.at[me], tp=jnp.where(z == 0, 1, tp - 2))
+
+    def piece_peer(q):
+        place = piece_place(me)
+        return remote(place, place, peer_sem.at[q], far_sem.at[me], ctx=2 * q + core)
+
+    def piece_pair(q):
+        place = piece_place(2 * q + core)
+        return remote(place, place, pair_sem.at[q], far_sem.at[2 * q + core], ctx=sibling)
+
+    def piece_wait(j):
+        remote(piece_place(j), piece_place(j), piece_sem, far_sem.at[j], ctx=sibling).wait_recv()
+
+    if paired:
+        pl.when(outer)(lambda: piece_down().start())
+
+    def send_own(c):
+        pl.when(has_left)(lambda: own_copy(c, 0).start())
+        pl.when(has_right)(lambda: own_copy(c, 1).start())
+
+    each(count, send_own)
+    load_up.wait()
+    load_w.wait()
+
+    def own_term(c):
+        acc[rows_of(c)] = term(z, c)
+
+    each(count, own_term)
+
+    if paired:
+
+        @pl.when(inner)
+        def _():
+            piece_wait(me)
+            for q in range(chips):
+                pl.when(q != chip)(lambda q=q: piece_peer(q).start())
+            piece_pair(chip).start()
+
+    load_bc.wait()
+    earlier = lax.broadcasted_iota(jnp.int32, (CHUNK, CHUNK), 0)
+    upto = jnp.where(earlier <= lax.broadcasted_iota(jnp.int32, (CHUNK, CHUNK), 1), 1.0, 0.0)
+
+    def weigh(c, before):
+        logs = log_ref[:, rows_of(c)]
+        cumlog = before + jnp.dot(
+            logs, upto, precision=lax.Precision.HIGHEST, preferred_element_type=F32
+        )
+        decay = jnp.exp(cumlog)
+        for h in range(heads):
+            c_rows = bc_ref[rows_of(c), h * 128 : (h + 1) * 128].astype(F32).T[STATE:]
+            weighted[h * STATE : (h + 1) * STATE, rows_of(c)] = (c_rows * decay[h : h + 1]).astype(BF16)
+        return cumlog[:, CHUNK - 1 : CHUNK]
+
+    part_decay = jnp.exp(lax.fori_loop(0, count, weigh, jnp.zeros((heads, 1), F32)))
     for h in range(heads):
-        c_rows = bc_ref[:, h * 128 + STATE : (h + 1) * 128]
-        dy = dy_ref[:, h * 128 : (h + 1) * 128]
-        term = later_terms(c_rows, dy, decay[:, h : h + 1])
-        out_ref[h] = decay[BLOCK - 1 : BLOCK, h : h + 1] * out_ref[h] + term
+        part[h, :STATE] = jnp.zeros((STATE, HEAD_DIM), F32)
+        part[h, STATE:] = jnp.broadcast_to(part_decay[h : h + 1], (8, HEAD_DIM))
+
+    def finish(c, total):
+        low_total = total.astype(BF16)
+        dy_ref[rows_of(c)] = low_total
+        for h in range(heads):
+            part[h, :STATE] += jnp.dot(
+                weighted[h * STATE : (h + 1) * STATE, rows_of(c)],
+                low_total[:, h * 128 : (h + 1) * 128],
+                preferred_element_type=F32,
+            )
+
+    if paired:
+        end = jnp.where(z == 1, 0, 3)
+        mate, far = 3 - z, 3 - end
+        next_in = jnp.where(z == 0, 1, tp - 2)
+
+        def sum_copy(c):
+            return remote(
+                sum_out.at[rows_of(c)], sum_in.at[rows_of(c)], sum_send.at[c], sum_recv.at[c], tp=end
+            )
+
+        def first_hop(c):
+            relay(end, c, mate).wait_recv()
+            relay(end, c, mate).start()
+            relay(mate, c, mate).wait_recv()
+            acc[rows_of(c)] += term(end, c) + term(mate, c)
+
+        def second_hop(c):
+            relay(far, c, mate).wait_recv()
+            outward = lax.dot_general(
+                got[low, rows_of(c)], far_w[:, :depth], LANES, preferred_element_type=F32
+            )
+            outward += lax.dot_general(
+                got[low + 1, rows_of(c)], far_w[:, depth:], LANES, preferred_element_type=F32
+            )
+            sum_out[rows_of(c)] = outward.astype(BF16)
+            sum_copy(c).start()
+            finish(c, acc[rows_of(c)] + term(far, c))
+
+        @pl.when(inner)
+        def _():
+            each(count // 2, first_hop)
+            for q in range(chips):
+
+                @pl.when(q != chip)
+                def _():
+                    piece_wait(2 * q + core)
+                    piece_pair(q).start()
+
+            each(count - count // 2, lambda c: first_hop(c + count // 2))
+            for q in range(chips):
+                piece_wait(2 * q + 1 - core)
+            each(count, second_hop)
+
+        def one_hop(c):
+            relay(next_in, c, next_in).wait_recv()
+            acc[rows_of(c)] += term(next_in, c)
+
+        def last_sum(c):
+            sum_copy(c).wait_recv()
+            finish(c, acc[rows_of(c)] + sum_in[rows_of(c)].astype(F32))
+
+        @pl.when(outer)
+        def _():
+            each(count, one_hop)
+            each(count, last_sum)
+
+    else:
+        for d in range(1, tp):
+
+            def hop(c):
+                @pl.when(z >= d)
+                def _():
+                    relay(z - d, c, z + 1).wait_recv()
+                    pl.when(has_right)(lambda: relay(z - d, c, z + 1).start())
+                    acc[rows_of(c)] += term(z - d, c)
+
+                @pl.when(z + d < tp)
+                def _():
+                    relay(z + d, c, z - 1).wait_recv()
+                    pl.when(has_left)(lambda: relay(z + d, c, z - 1).start())
+                    acc[rows_of(c)] += term(z + d, c)
+
+            each(count, hop)
+        each(count, lambda c: finish(c, acc[rows_of(c)]))
+
+    swap = remote(part, sib_part, swap_sem.at[0], swap_sem.at[1], ctx=sibling)
+    swap.start()
+    swap.wait_recv()
+    for j in range(half):
+        mine, other = part[core * half + j], sib_part[core * half + j]
+        first, second = jnp.where(core == 0, mine, other), jnp.where(core == 0, other, mine)
+        message[j] = part_combined(first, second)
+
+    def chip_copy(q):
+        return remote(message, later.at[chip], chip_send.at[q], chip_recv.at[chip], ctx=2 * q + core)
+
+    for q in reversed(range(chips)):
+        pl.when(q < chip)(lambda q=q: chip_copy(q).start())
+    half_in[...] = jnp.zeros_like(half_in)
+    for q in reversed(range(chips)):
+
+        @pl.when(q > chip)
+        def _():
+            remote(message, later.at[q], chip_send.at[q], chip_recv.at[q], ctx=sibling).wait_recv()
+            for j in range(half):
+                half_in[j] = later[q, j, :STATE] + later[q, j, STATE : STATE + 1] * half_in[j]
+
+    hand_over = remote(half_in, sib_half, swap_sem.at[2], swap_sem.at[3], ctx=sibling)
+    hand_over.start()
+    hand_over.wait_recv()
+    for j in range(half):
+        for h, total in ((core * half + j, half_in[j]), ((1 - core) * half + j, sib_half[j])):
+            nearer = sib_part[h, :STATE] + sib_part[h, STATE : STATE + 1] * total
+            in_ref[h] = jnp.where(core == 1, total, nearer)
+
+    def own_sent(c):
+        pl.when(has_left)(lambda: own_copy(c, 0).wait_send())
+        pl.when(has_right)(lambda: own_copy(c, 1).wait_send())
+
+    each(count, own_sent)
+    if paired:
+
+        @pl.when(inner)
+        def _():
+            for q in range(chips):
+                pl.when(q != chip)(lambda q=q: piece_peer(q).wait_send())
+                piece_pair(q).wait_send()
+
+            def passed(c):
+                relay(end, c, mate).wait_send()
+                sum_copy(c).wait_send()
+
+            each(count, passed)
+
+        pl.when(outer)(lambda: piece_down().wait_send())
+    else:
+        for d in range(1, tp):
+
+            def passed(c):
+                pl.when(jnp.logical_and(z >= d, has_right))(lambda: relay(z - d, c, z + 1).wait_send())
+                pl.when(jnp.logical_and(z + d < tp, has_left))(lambda: relay(z + d, c, z - 1).wait_send())
+
+            each(count, passed)
+    swap.wait_send()
+    for q in range(chips):
+        pl.when(q < chip)(lambda q=q: chip_copy(q).wait_send())
+    hand_over.wait_send()
+
+
+def projected(upstream, out_weight, head_bc, log_decay):
+    tp, ctx = lax.axis_size("tp"), lax.axis_size("ctx")
+    tokens, depth = upstream.shape
+    heads = log_decay.shape[0]
+    width, chips, count = heads * HEAD_DIM, ctx // 2, tokens // CHUNK
+    paired = tp == 4
+    dma = pltpu.SemaphoreType.DMA
+    anywhere = pl.BlockSpec(memory_space=pl.ANY)
+    vmem = pl.BlockSpec(memory_space=pltpu.VMEM)
+    packed = STATE + 8
+    sums = (tokens, width) if paired else (16, 128)
+    return pl.pallas_call(
+        functools.partial(project_kernel, tp, ctx),
+        out_shape=(
+            jax.ShapeDtypeStruct((tokens, width), BF16),
+            jax.ShapeDtypeStruct((heads, STATE, HEAD_DIM), F32),
+        ),
+        in_specs=[anywhere, anywhere, anywhere, vmem],
+        out_specs=(vmem, vmem),
+        scratch_shapes=[
+            pltpu.VMEM((tp, tokens, depth), BF16),
+            pltpu.VMEM(out_weight.shape, BF16),
+            pltpu.VMEM(head_bc.shape, BF16),
+            pltpu.VMEM((width, 2 * depth) if paired else (16, 128), BF16),
+            pltpu.VMEM((tokens, width), F32),
+            pltpu.VMEM(sums, BF16),
+            pltpu.VMEM(sums, BF16),
+            pltpu.VMEM((heads * STATE, tokens), BF16),
+            pltpu.VMEM((heads, packed, HEAD_DIM), F32),
+            pltpu.VMEM((heads, packed, HEAD_DIM), F32),
+            pltpu.VMEM((heads // 2, packed, HEAD_DIM), F32),
+            pltpu.VMEM((chips, heads // 2, packed, HEAD_DIM), F32),
+            pltpu.VMEM((heads // 2, STATE, HEAD_DIM), F32),
+            pltpu.VMEM((heads // 2, STATE, HEAD_DIM), F32),
+            dma((3,)),
+            dma((2, count)),
+            dma((tp, count)),
+            dma((tp, count)),
+            dma((count,)),
+            dma((count,)),
+            dma,
+            dma((chips,)),
+            dma((chips,)),
+            dma((ctx,)),
+            dma((4,)),
+            dma((chips,)),
+            dma((chips,)),
+        ],
+        compiler_params=pltpu.CompilerParams(
+            collective_id=0, has_side_effects=True, vmem_limit_bytes=56 * 1024 * 1024
+        ),
+        name="project_and_exchange",
+    )(upstream, out_weight, head_bc, log_decay)
 
 
 def block_kernel(
@@ -95,43 +461,17 @@
     )
 
 
-def later_state(part, part_log, axis):
-    count, place = lax.axis_size(axis), lax.axis_index(axis)
-    parts = lax.all_gather(part, axis)
-    logs = lax.all_gather(part_log, axis)
-    ids = jnp.arange(count)[:, None]
-    between = jnp.where(ids > place, logs, 0.0)
-    before = jnp.cumsum(between, axis=0) - between
-    weights = jnp.where(ids > place, jnp.exp(before), 0.0)
-    return jnp.sum(weights[:, :, None, None] * parts, axis=0)
-
-
 def per_device(upstream, out_weight, inner_act, head_bc, log_decay, states, skip):
     tokens, heads = inner_act.shape[0], log_decay.shape[0]
     width = heads * HEAD_DIM
     blocks = tokens // BLOCK
-    out_grad = lax.dot_general(
-        lax.all_gather(upstream, "tp", axis=1, tiled=True),
-        out_weight,
-        LANES,
-        preferred_element_type=F32,
-    ).astype(BF16)
+    out_grad, incoming = projected(upstream, out_weight, head_bc, log_decay)
     wide = pl.BlockSpec((BLOCK, width), lambda i: (blocks - 1 - i, 0))
     logs = pl.BlockSpec((heads, BLOCK), lambda i: (0, blocks - 1 - i))
     carry = pl.BlockSpec((heads, STATE, HEAD_DIM), lambda i: (0, 0, 0))
     params = pltpu.CompilerParams(
         dimension_semantics=("arbitrary",), vmem_limit_bytes=48 * 1024 * 1024
     )
-    part = pl.pallas_call(
-        functools.partial(terms_kernel, heads),
-        out_shape=jax.ShapeDtypeStruct((heads, STATE, HEAD_DIM), F32),
-        grid=(blocks,),
-        in_specs=[wide, wide, logs],
-        out_specs=carry,
-        compiler_params=params,
-        name="part_terms",
-    )(head_bc, out_grad, log_decay)
-    incoming = later_state(part, jnp.sum(log_decay, axis=1), "ctx")
     return pl.pallas_call(
         functools.partial(block_kernel, heads),
         out_shape=(

time: 243 us -> 149 us (0.61)
  waiting for transfers between devices: 165 us -> 0 us
  Pallas kernels: 29.1 us -> 147 us
  between operations: 14.8 us -> 0.73 us
  blocking collectives: 13.9 us -> 0 us
  matrix products: 13.7 us -> 0 us
  local copies, waits for them, and re-layouts: 3.86 us -> 0.96 us
    all_gather x2 -> x0, waiting for transfers between devices: 164 us -> none  [the longest x1 154 us: per_device(): lax.all_gather(upstream, 'tp', axis=1, tiled=True)]
    pallas_call x1, Pallas kernels: 6.74 us -> 124 us  [projected(): pl.pallas_call(functools.partial(project_kernel, tp, ctx), out_shape=(jax...]
    unnamed x1 -> x0, blocking collectives: 13.9 us -> none
    dot_general x1 -> x0, matrix products: 13.7 us -> none  [per_device(): lax.dot_general(lax.all_gather(upstream, 'tp', axis=1, tiled=True), out_w...]
    unnamed x17 -> x12, local copies, waits for them, and re-layouts: 3.78 us -> 0.96 us
  transfers between devices with their start and end apart: 2 -> 0, of which waited for: 2 -> 0; matrix products, arithmetic and copies ran while one was open for 1% -> 0% of each run, Pallas kernels for 0% -> 0%
where the time goes in v1:
time: 149 us; the launch traced here: 148 us
  Pallas kernels  147 us (99%)
    pallas_call x1, Pallas kernels, projected(): pl.pallas_call(functools.partial(project_kernel, tp, ctx), out_shape=(jax...  124 us
    pallas_call x1, Pallas kernels, per_device(): pl.pallas_call(functools.partial(block_kernel, heads), out_shape=(jax.Sha...  22.3 us

profile of v1, /device:TPU:0, one launch (start us, length us, event | category | flops | bytes accessed | tf_op | source)
XLA Modules:
  0.0 148.4 jit_solution(13843401311142625845)
XLA Ops:
  0.6 0.0 copy-start.4
  0.6 0.0 copy-start
  0.7 0.0 copy-start.5
  0.7 0.0 copy-start.2
  0.7 0.0 copy-start.1
  0.7 124.5 %project_and_exchange.1 = (bf16[1024,1024]{1,0:T(8,128)(2,1)}, f32[8,64,128]{2,1,0:T(8,128)}) custom-call(bf16[1024,1024]{1,0:T(8,128)(2,1)} %up_hbm.1, bf16[1024,4096]{1,0:T(8,128)(2,1)} %w_hbm.1, bf16[1024,1024]{1,0:T(8,128)(2,1)} %bc_ref.1, f32[8,1024]{1,0:T(8,128)} %log_ref.3), custom_call_target="tpu_custom_call" | custom-call | tf_op jit(solution)/shard_map/project_and_exchange/pallas_call | solution.py:368
  125.2 0.0 copy-done.4
  125.2 0.0 copy-done
  125.2 0.0 copy-done.5
  125.2 0.0 copy-done.2
  125.2 0.0 copy-done.1
  125.2 0.0 copy-start.3
  125.2 0.9 copy-done.3
  126.2 22.3 %block_gradients.1 = (bf16[1024,1024]{1,0:T(8,128)(2,1)}, f32[1024,1024]{1,0:T(8,128)}, f32[8,1024]{1,0:T(8,128)}) custom-call(bf16[1024,1024]{1,0:T(8,128)(2,1)S(1)} %copy-done.1, bf16[1024,1024]{1,0:T(8,128)(2,1)S(1)} %copy-done, bf16[1024,1024]{1,0:T(8,128)(2,1)} %get-tuple-element.5.dy_ref, f32[8,1024]{1,0:T(8,128)S(1)} %copy-done.4, ...), custom_call_target="tpu_custom_call" | custom-call | tf_op jit(solution)/shard_map/block_gradients/pallas_call | solution.py:475
Async XLA Ops:
  0.6 124.5 %copy-start.4 = (f32[8,1024]{1,0:T(8,128)S(1)}, f32[8,1024]{1,0:T(8,128)}, u32[]{:S(2)}) copy-start(f32[8,1024]{1,0:T(8,128)} %log_ref.3) | copy-start | bytes 98308
  0.6 124.5 %copy-start = (bf16[1024,1024]{1,0:T(8,128)(2,1)S(1)}, bf16[1024,1024]{1,0:T(8,128)(2,1)}, u32[]{:S(2)}) copy-start(bf16[1024,1024]{1,0:T(8,128)(2,1)} %bc_ref.1) | copy-start | bytes 6291460
  0.7 124.5 %copy-start.5 = (f32[8]{0:T(128)S(1)}, f32[8]{0:T(128)}, u32[]{:S(2)}) copy-start(f32[8]{0:T(128)} %skip_ref.1) | copy-start | bytes 100
  0.7 124.5 %copy-start.2 = (f32[4,8,64,128]{3,2,1,0:T(8,128)S(1)}, f32[4,8,64,128]{3,2,1,0:T(8,128)}, u32[]{:S(2)}) copy-start(f32[4,8,64,128]{3,2,1,0:T(8,128)} %s_ref.1) | copy-start | bytes 3145732
  0.7 124.5 %copy-start.1 = (bf16[1024,1024]{1,0:T(8,128)(2,1)S(1)}, bf16[1024,1024]{1,0:T(8,128)(2,1)}, u32[]{:S(2)}) copy-start(bf16[1024,1024]{1,0:T(8,128)(2,1)} %x_ref.1) | copy-start | bytes 6291460
  125.2 1.0 copy-start.3

commit v2 on v1

--- a/solution.py
+++ b/solution.py
@@ -10,7 +10,8 @@
 HEAD_DIM = 128
 STATE = 64
 BLOCK = 256
-CHUNK = 128
+CHUNK = 64
+PER = BLOCK // CHUNK
 F32 = jnp.float32
 BF16 = jnp.bfloat16
 ROWS = (((0,), (0,)), ((), ()))
@@ -23,11 +24,6 @@
     upto = jnp.where(earlier <= later, 1.0, 0.0)
     rows = jnp.dot(log_rows, upto, precision=lax.Precision.HIGHEST, preferred_element_type=F32)
     return rows, rows.T
-
-
-def later_terms(c_rows, dy, head_decay):
-    weighted = (c_rows.astype(F32) * head_decay).astype(BF16)
-    return lax.dot_general(weighted, dy, ROWS, preferred_element_type=F32)
 
 
 def part_combined(first, second):
@@ -43,7 +39,12 @@
     w_hbm,
     bc_hbm,
     log_ref,
-    dy_ref,
+    x_hbm,
+    s_hbm,
+    skip_ref,
+    gx_hbm,
+    gbc_hbm,
+    term_hbm,
     in_ref,
     got,
     w_ref,
@@ -53,6 +54,14 @@
     sum_out,
     sum_in,
     weighted,
+    x_ref,
+    s_ref,
+    dy_ref,
+    gx_ref,
+    gbc_ref,
+    term_ref,
+    cum_rows,
+    cum_cols,
     part,
     sib_part,
     message,
@@ -72,6 +81,7 @@
     swap_sem,
     chip_send,
     chip_recv,
+    out_sem,
 ):
     z, me = lax.axis_index("tp"), lax.axis_index("ctx")
     core, chip = lax.rem(me, 2), lax.div(me, 2)
@@ -83,6 +93,7 @@
     width = w_hbm.shape[0]
     piece = width // ctx
     count = tokens // CHUNK
+    blocks = tokens // BLOCK
     paired = tp == 4
     has_left, has_right = z > 0, z < tp - 1
     inner = jnp.logical_and(has_left, has_right)
@@ -124,6 +135,10 @@
     load_up.start()
     load_w.start()
     load_bc.start()
+    load_x = pltpu.make_async_copy(x_hbm, x_ref, local_sem.at[3])
+    load_s = pltpu.make_async_copy(s_hbm, s_ref, local_sem.at[4])
+    load_x.start()
+    load_s.start()
 
     barrier = pltpu.get_barrier_semaphore()
 
@@ -164,8 +179,9 @@
         pl.when(outer)(lambda: piece_down().start())
 
     def send_own(c):
-        pl.when(has_left)(lambda: own_copy(c, 0).start())
-        pl.when(has_right)(lambda: own_copy(c, 1).start())
+        early = jnp.logical_or(c < count // 2, not paired)
+        pl.when(jnp.logical_and(has_left, jnp.logical_or(early, z != 2)))(lambda: own_copy(c, 0).start())
+        pl.when(jnp.logical_and(has_right, jnp.logical_or(early, z != 1)))(lambda: own_copy(c, 1).start())
 
     each(count, send_own)
     load_up.wait()
@@ -186,34 +202,76 @@
             piece_pair(chip).start()
 
     load_bc.wait()
-    earlier = lax.broadcasted_iota(jnp.int32, (CHUNK, CHUNK), 0)
-    upto = jnp.where(earlier <= lax.broadcasted_iota(jnp.int32, (CHUNK, CHUNK), 1), 1.0, 0.0)
-
-    def weigh(c, before):
-        logs = log_ref[:, rows_of(c)]
-        cumlog = before + jnp.dot(
-            logs, upto, precision=lax.Precision.HIGHEST, preferred_element_type=F32
-        )
-        decay = jnp.exp(cumlog)
+
+    def rows_of_block(b):
+        return pl.ds(pl.multiple_of(b * BLOCK, BLOCK), BLOCK)
+
+    def weigh(b):
+        here = rows_of_block(b)
+        rows, cols = cumulative(log_ref[:, here])
+        cum_rows[:, here] = rows
+        cum_cols[here] = cols
+        decay = jnp.exp(rows)
         for h in range(heads):
-            c_rows = bc_ref[rows_of(c), h * 128 : (h + 1) * 128].astype(F32).T[STATE:]
-            weighted[h * STATE : (h + 1) * STATE, rows_of(c)] = (c_rows * decay[h : h + 1]).astype(BF16)
-        return cumlog[:, CHUNK - 1 : CHUNK]
-
-    part_decay = jnp.exp(lax.fori_loop(0, count, weigh, jnp.zeros((heads, 1), F32)))
-    for h in range(heads):
-        part[h, :STATE] = jnp.zeros((STATE, HEAD_DIM), F32)
-        part[h, STATE:] = jnp.broadcast_to(part_decay[h : h + 1], (8, HEAD_DIM))
-
-    def finish(c, total):
-        low_total = total.astype(BF16)
-        dy_ref[rows_of(c)] = low_total
+            c_rows = bc_ref[here, h * 128 : (h + 1) * 128].astype(F32).T[STATE:]
+            weighted[h * STATE : (h + 1) * STATE, here] = (c_rows * decay[h : h + 1]).astype(BF16)
+
+    each(blocks, weigh)
+    load_x.wait()
+    load_s.wait()
+
+    def block_terms(b):
+        here = rows_of_block(b)
         for h in range(heads):
-            part[h, :STATE] += jnp.dot(
-                weighted[h * STATE : (h + 1) * STATE, rows_of(c)],
-                low_total[:, h * 128 : (h + 1) * 128],
+            term_ref[b, h] = jnp.dot(
+                weighted[h * STATE : (h + 1) * STATE, here],
+                dy_ref[here, h * 128 : (h + 1) * 128],
                 preferred_element_type=F32,
             )
+
+    k_ids = lax.broadcasted_iota(jnp.int32, (BLOCK, BLOCK), 0)
+    q_ids = lax.broadcasted_iota(jnp.int32, (BLOCK, BLOCK), 1)
+
+    def local_gradients(b, group):
+        here = rows_of_block(b)
+        for h in range(group * heads // PER, (group + 1) * heads // PER):
+            at = slice(h * 128, (h + 1) * 128)
+            bc, x, dy = bc_ref[here, at], x_ref[here, at], dy_ref[here, at]
+            b_rows, c_rows = bc[:, :STATE], bc[:, STATE:]
+            column = cum_cols[here, h : h + 1]
+            gap = cum_rows[h : h + 1, here] - column
+            gate = jnp.exp(jnp.where(q_ids >= k_ids, gap, -1e30))
+            scores = lax.dot_general(b_rows, c_rows, LANES, preferred_element_type=F32) * gate
+            inside = lax.dot_general(x, dy, LANES, preferred_element_type=F32) * gate
+            scores, inside = scores.astype(BF16), inside.astype(BF16)
+            gx = jnp.dot(scores, dy, preferred_element_type=F32)
+            gx_ref[here, at] = gx + skip_ref[h] * dy.astype(F32)
+            gb = jnp.dot(inside, c_rows, preferred_element_type=F32)
+            gc = lax.dot_general(inside, b_rows, ROWS, preferred_element_type=F32)
+            start = s_ref[b, h].astype(BF16)
+            gc += jnp.exp(column) * lax.dot_general(dy, start, LANES, preferred_element_type=F32)
+            gbc_ref[here, at] = jnp.concatenate([gb, gc], axis=1)
+
+    def out_copies(b):
+        here = rows_of_block(b)
+        return (
+            pltpu.make_async_copy(gx_ref.at[here], gx_hbm.at[here], out_sem.at[0, b]),
+            pltpu.make_async_copy(gbc_ref.at[here], gbc_hbm.at[here], out_sem.at[1, b]),
+        )
+
+    def send_out(b):
+        for copy in out_copies(b):
+            copy.start()
+
+    def drain(arrive):
+        def take(b):
+            for i in range(PER):
+                dy_ref[rows_of(b * PER + i)] = arrive(b, b * PER + i).astype(BF16)
+                pl.when(b > 0)(functools.partial(local_gradients, b - 1, i))
+            pl.when(b > 0)(lambda: send_out(b - 1))
+            block_terms(b)
+
+        each(blocks, take)
 
     if paired:
         end = jnp.where(z == 1, 0, 3)
@@ -228,10 +286,18 @@
         def first_hop(c):
             relay(end, c, mate).wait_recv()
             relay(end, c, mate).start()
+
+            @pl.when(c < count - count // 2)
+            def _():
+                pl.when(z == 2)(lambda: own_copy(c + count // 2, 0).start())
+                pl.when(z == 1)(lambda: own_copy(c + count // 2, 1).start())
+
+            acc[rows_of(c)] += term(end, c)
+
+        def second_hop(b, c):
+            early = c + count // 2
+            pl.when(early < count)(lambda: first_hop(early))
             relay(mate, c, mate).wait_recv()
-            acc[rows_of(c)] += term(end, c) + term(mate, c)
-
-        def second_hop(c):
             relay(far, c, mate).wait_recv()
             outward = lax.dot_general(
                 got[low, rows_of(c)], far_w[:, :depth], LANES, preferred_element_type=F32
@@ -241,7 +307,7 @@
             )
             sum_out[rows_of(c)] = outward.astype(BF16)
             sum_copy(c).start()
-            finish(c, acc[rows_of(c)] + term(far, c))
+            return acc[rows_of(c)] + term(mate, c) + term(far, c)
 
         @pl.when(inner)
         def _():
@@ -253,23 +319,22 @@
                     piece_wait(2 * q + core)
                     piece_pair(q).start()
 
-            each(count - count // 2, lambda c: first_hop(c + count // 2))
             for q in range(chips):
                 piece_wait(2 * q + 1 - core)
-            each(count, second_hop)
+            drain(second_hop)
 
         def one_hop(c):
             relay(next_in, c, next_in).wait_recv()
             acc[rows_of(c)] += term(next_in, c)
 
-        def last_sum(c):
+        def last_sum(b, c):
             sum_copy(c).wait_recv()
-            finish(c, acc[rows_of(c)] + sum_in[rows_of(c)].astype(F32))
+            return acc[rows_of(c)] + sum_in[rows_of(c)].astype(F32)
 
         @pl.when(outer)
         def _():
             each(count, one_hop)
-            each(count, last_sum)
+            drain(last_sum)
 
     else:
         for d in range(1, tp):
@@ -288,10 +353,23 @@
                     acc[rows_of(c)] += term(z + d, c)
 
             each(count, hop)
-        each(count, lambda c: finish(c, acc[rows_of(c)]))
+        drain(lambda b, c: acc[rows_of(c)])
+
+    for h in range(heads):
+        total, decay = term_ref[blocks - 1, h], 0.0
+        for b in reversed(range(blocks)):
+            log = cum_rows[h : h + 1, (b + 1) * BLOCK - 1 : (b + 1) * BLOCK]
+            decay = decay + log
+            if b < blocks - 1:
+                total = term_ref[b, h] + jnp.exp(log) * total
+        part[h, :STATE] = total
+        part[h, STATE:] = jnp.broadcast_to(jnp.exp(decay), (8, HEAD_DIM))
+    term_copy = pltpu.make_async_copy(term_ref, term_hbm, local_sem.at[5])
+    term_copy.start()
 
     swap = remote(part, sib_part, swap_sem.at[0], swap_sem.at[1], ctx=sibling)
     swap.start()
+    local_gradients(blocks - 1, 0)
     swap.wait_recv()
     for j in range(half):
         mine, other = part[core * half + j], sib_part[core * half + j]
@@ -304,6 +382,8 @@
     for q in reversed(range(chips)):
         pl.when(q < chip)(lambda q=q: chip_copy(q).start())
     half_in[...] = jnp.zeros_like(half_in)
+    local_gradients(blocks - 1, 1)
+    local_gradients(blocks - 1, 2)
     for q in reversed(range(chips)):
 
         @pl.when(q > chip)
@@ -314,6 +394,8 @@
 
     hand_over = remote(half_in, sib_half, swap_sem.at[2], swap_sem.at[3], ctx=sibling)
     hand_over.start()
+    local_gradients(blocks - 1, 3)
+    send_out(blocks - 1)
     hand_over.wait_recv()
     for j in range(half):
         for h, total in ((core * half + j, half_in[j]), ((1 - core) * half + j, sib_half[j])):
@@ -352,9 +434,13 @@
     for q in range(chips):
         pl.when(q < chip)(lambda q=q: chip_copy(q).wait_send())
     hand_over.wait_send()
-
-
-def projected(upstream, out_weight, head_bc, log_decay):
+    term_copy.wait()
+    for b in range(blocks):
+        for copy in out_copies(b):
+            copy.wait()
+
+
+def projected(upstream, out_weight, inner_act, head_bc, log_decay, states, skip):
     tp, ctx = lax.axis_size("tp"), lax.axis_size("ctx")
     tokens, depth = upstream.shape
     heads = log_decay.shape[0]
@@ -368,11 +454,21 @@
     return pl.pallas_call(
         functools.partial(project_kernel, tp, ctx),
         out_shape=(
-            jax.ShapeDtypeStruct((tokens, width), BF16),
+            jax.ShapeDtypeStruct((tokens, width), F32),
+            jax.ShapeDtypeStruct((tokens, width), F32),
+            jax.ShapeDtypeStruct(states.shape, F32),
             jax.ShapeDtypeStruct((heads, STATE, HEAD_DIM), F32),
         ),
-        in_specs=[anywhere, anywhere, anywhere, vmem],
-        out_specs=(vmem, vmem),
+        in_specs=[
+            anywhere,
+            anywhere,
+            anywhere,
+            vmem,
+            anywhere,
+            anywhere,
+            pl.BlockSpec(memory_space=pltpu.SMEM),
+        ],
+        out_specs=(anywhere, anywhere, anywhere, vmem),
         scratch_shapes=[
             pltpu.VMEM((tp, tokens, depth), BF16),
             pltpu.VMEM(out_weight.shape, BF16),
@@ -382,13 +478,21 @@
             pltpu.VMEM(sums, BF16),
             pltpu.VMEM(sums, BF16),
             pltpu.VMEM((heads * STATE, tokens), BF16),
+            pltpu.VMEM((tokens, width), BF16),
+            pltpu.VMEM(states.shape, F32),
+            pltpu.VMEM((tokens, width), BF16),
+            pltpu.VMEM((tokens, width), F32),
+            pltpu.VMEM((tokens, width), F32),
+            pltpu.VMEM(states.shape, F32),
+            pltpu.VMEM((heads, tokens), F32),
+            pltpu.VMEM((tokens, heads), F32),
             pltpu.VMEM((heads, packed, HEAD_DIM), F32),
             pltpu.VMEM((heads, packed, HEAD_DIM), F32),
             pltpu.VMEM((heads // 2, packed, HEAD_DIM), F32),
             pltpu.VMEM((chips, heads // 2, packed, HEAD_DIM), F32),
             pltpu.VMEM((heads // 2, STATE, HEAD_DIM), F32),
             pltpu.VMEM((heads // 2, STATE, HEAD_DIM), F32),
-            dma((3,)),
+            dma((6,)),
             dma((2, count)),
             dma((tp, count)),
             dma((tp, count)),
@@ -401,27 +505,25 @@
             dma((4,)),
             dma((chips,)),
             dma((chips,)),
+            dma((2, tokens // BLOCK)),
         ],
         compiler_params=pltpu.CompilerParams(
             collective_id=0, has_side_effects=True, vmem_limit_bytes=56 * 1024 * 1024
         ),
         name="project_and_exchange",
-    )(upstream, out_weight, head_bc, log_decay)
-
-
-def block_kernel(
-    heads, x_ref, bc_ref, dy_ref, log_ref, s_ref, skip_ref, in_ref, gx_ref, gbc_ref, glog_ref, h_ref
+    )(upstream, out_weight, head_bc, log_decay, inner_act, states, skip)
+
+
+def closing_kernel(
+    heads, x_ref, bc_ref, gx0_ref, gbc0_ref, log_ref, s_ref, term_ref, in_ref, gx_ref, gbc_ref, glog_ref, h_ref
 ):
     @pl.when(pl.program_id(0) == 0)
     def _():
         h_ref[...] = in_ref[...]
 
     rows, cols = cumulative(log_ref[...])
-    decay = jnp.exp(cols)
-    tail = jnp.exp(cols[BLOCK - 1 : BLOCK, :] - cols)
-    k_ids = lax.broadcasted_iota(jnp.int32, (BLOCK, BLOCK), 0)
-    q_ids = lax.broadcasted_iota(jnp.int32, (BLOCK, BLOCK), 1)
-    causal = q_ids >= k_ids
+    last = cols[BLOCK - 1 : BLOCK, :]
+    whole, tail = jnp.exp(last), jnp.exp(last - cols)
     sign = jnp.where(lax.broadcasted_iota(jnp.int32, (1, 128), 1) < STATE, -1.0, 1.0)
     lane = lax.broadcasted_iota(jnp.int32, (BLOCK, heads), 1)
     token = lax.broadcasted_iota(jnp.int32, (BLOCK, 1), 0)
@@ -429,33 +531,24 @@
     for h in range(heads):
         here = slice(h * 128, (h + 1) * 128)
         bc = bc_ref[:, here]
-        b_rows, c_rows = bc[:, :STATE], bc[:, STATE:]
-        x, dy = x_ref[:, here], dy_ref[:, here]
-        carried, start = h_ref[h], s_ref[0, h]
-        held, start_low = carried.astype(BF16), start.astype(BF16)
-        gap = rows[h : h + 1, :] - cols[:, h : h + 1]
-        gate = jnp.exp(jnp.where(causal, gap, -1e30))
-        scores = lax.dot_general(b_rows, c_rows, LANES, preferred_element_type=F32) * gate
-        inner = lax.dot_general(x, dy, LANES, preferred_element_type=F32) * gate
-        scores, inner = scores.astype(BF16), inner.astype(BF16)
-        tail_h, decay_h = tail[:, h : h + 1], decay[:, h : h + 1]
-        gx = jnp.dot(scores, dy, preferred_element_type=F32)
-        gx += tail_h * jnp.dot(b_rows, held, preferred_element_type=F32)
-        gx += skip_ref[h] * dy.astype(F32)
-        gx_ref[:, here] = gx.astype(BF16)
-        gb_tail = tail_h * lax.dot_general(x, held, LANES, preferred_element_type=F32)
-        gb = jnp.dot(inner, c_rows, preferred_element_type=F32) + gb_tail
-        gc = lax.dot_general(inner, b_rows, ROWS, preferred_element_type=F32)
-        gc += decay_h * lax.dot_general(dy, start_low, LANES, preferred_element_type=F32)
-        gbc = jnp.concatenate([gb, gc], axis=1)
+        carried = h_ref[h]
+        held = carried.astype(BF16)
+        tail_h, whole_h = tail[:, h : h + 1], whole[:, h : h + 1]
+        added = jnp.dot(bc[:, :STATE], held, preferred_element_type=F32)
+        gx_ref[:, here] = (gx0_ref[:, here] + tail_h * added).astype(BF16)
+        gb_tail = tail_h * lax.dot_general(x_ref[:, here], held, LANES, preferred_element_type=F32)
+        wide_tail = jnp.concatenate([gb_tail, jnp.zeros_like(gb_tail)], axis=1)
+        gbc = gbc0_ref[:, here] + wide_tail
         gbc_ref[:, here] = gbc
-        dcum_h = jnp.sum(bc.astype(F32) * gbc * sign, axis=1, keepdims=True)
-        whole = decay[BLOCK - 1 : BLOCK, h : h + 1]
-        at_end = whole * jnp.sum(start * carried) + jnp.sum(b_rows.astype(F32) * gb_tail)
+        bc_wide = bc.astype(F32)
+        dcum_h = jnp.sum(bc_wide * gbc * sign, axis=1, keepdims=True)
+        at_end = whole_h * jnp.sum(s_ref[0, h] * carried) + jnp.sum(bc_wide * wide_tail)
         dcum_h = dcum_h + jnp.where(token == BLOCK - 1, at_end, 0.0)
         dcum = jnp.where(lane == h, dcum_h, dcum)
-        h_ref[h] = whole * carried + later_terms(c_rows, dy, decay_h)
-    from_here = jnp.where(k_ids >= q_ids, 1.0, 0.0)
+        h_ref[h] = whole_h * carried + term_ref[0, h]
+    s_ids = lax.broadcasted_iota(jnp.int32, (BLOCK, BLOCK), 0)
+    t_ids = lax.broadcasted_iota(jnp.int32, (BLOCK, BLOCK), 1)
+    from_here = jnp.where(s_ids >= t_ids, 1.0, 0.0)
     glog_ref[...] = jnp.dot(
         dcum.T, from_here, precision=lax.Precision.HIGHEST, preferred_element_type=F32
     )
@@ -465,15 +558,18 @@
     tokens, heads = inner_act.shape[0], log_decay.shape[0]
     width = heads * HEAD_DIM
     blocks = tokens // BLOCK
-    out_grad, incoming = projected(upstream, out_weight, head_bc, log_decay)
+    gx, gbc, terms, incoming = projected(
+        upstream, out_weight, inner_act, head_bc, log_decay, states, skip
+    )
     wide = pl.BlockSpec((BLOCK, width), lambda i: (blocks - 1 - i, 0))
     logs = pl.BlockSpec((heads, BLOCK), lambda i: (0, blocks - 1 - i))
+    block = pl.BlockSpec((1, heads, STATE, HEAD_DIM), lambda i: (blocks - 1 - i, 0, 0, 0))
     carry = pl.BlockSpec((heads, STATE, HEAD_DIM), lambda i: (0, 0, 0))
     params = pltpu.CompilerParams(
         dimension_semantics=("arbitrary",), vmem_limit_bytes=48 * 1024 * 1024
     )
     return pl.pallas_call(
-        functools.partial(block_kernel, heads),
+        functools.partial(closing_kernel, heads),
         out_shape=(
             jax.ShapeDtypeStruct((tokens, width), BF16),
             jax.ShapeDtypeStruct((tokens, width), F32),
@@ -484,16 +580,17 @@
             wide,
             wide,
             wide,
+            wide,
             logs,
-            pl.BlockSpec((1, heads, STATE, HEAD_DIM), lambda i: (blocks - 1 - i, 0, 0, 0)),
-            pl.BlockSpec(memory_space=pltpu.SMEM),
+            block,
+            block,
             carry,
         ],
         out_specs=(wide, wide, logs),
         scratch_shapes=[pltpu.VMEM((heads, STATE, HEAD_DIM), F32)],
         compiler_params=params,
-        name="block_gradients",
-    )(inner_act, head_bc, out_grad, log_decay, states, skip, incoming)
+        name="carried_terms",
+    )(inner_act, head_bc, gx, gbc, log_decay, states, terms, incoming)
 
 
 def solution(mesh):

time: 149 us -> 143 us (0.960)
  Pallas kernels: 147 us -> 140 us
    pallas_call x1, Pallas kernels: 22.3 us -> 11.7 us  [per_device(): pl.pallas_call(functools.partial(closing_kernel, heads), out_shape=(jax.S...]
    pallas_call x1, Pallas kernels: 124 us -> 128 us  [projected(): pl.pallas_call(functools.partial(project_kernel, tp, ctx), out_shape=(jax...]
where the time goes in v2:
time: 143 us
  Pallas kernels  140 us (98%)
  local copies, waits for them, and re-layouts  2.18 us (2%)
    pallas_call x1, Pallas kernels, projected(): pl.pallas_call(functools.partial(project_kernel, tp, ctx), out_shape=(jax...  128 us
    pallas_call x1, Pallas kernels, per_device(): pl.pallas_call(functools.partial(closing_kernel, heads), out_shape=(jax.S...  11.7 us

profile of v2, /device:TPU:0, one launch (start us, length us, event | category | flops | bytes accessed | tf_op | source)
XLA Modules:
  0.0 143.0 jit_solution(8723974543672833994)
XLA Ops:
  0.6 0.0 copy-start.1
  0.6 0.0 copy-start.4
  0.7 0.0 copy-start
  0.7 128.5 %project_and_exchange.1 = (f32[1024,1024]{1,0:T(8,128)}, f32[1024,1024]{1,0:T(8,128)}, f32[4,8,64,128]{3,2,1,0:T(8,128)}, f32[8,64,128]{2,1,0:T(8,128)}) custom-call(bf16[1024,1024]{1,0:T(8,128)(2,1)} %up_hbm.1, bf16[1024,4096]{1,0:T(8,128)(2,1)} %w_hbm.1, bf16[1024,1024]{1,0:T(8,128)(2,1)} %bc_ref.1, f32[8,1024]{1,0:T(8,128)} %log_ref.3, ...), custom_call_target="tpu_custom_call" | custom-call | tf_op jit(solution)/shard_map/project_and_exchange/pallas_call | solution.py:454
  129.1 0.0 copy-done.1
  129.1 0.0 copy-done.4
  129.1 0.0 copy-done
  129.2 0.0 copy-start.2
  129.2 1.2 copy-done.2
  130.4 0.0 copy-start.3
  130.4 0.9 copy-done.3
  131.3 11.7 %carried_terms.1 = (bf16[1024,1024]{1,0:T(8,128)(2,1)}, f32[1024,1024]{1,0:T(8,128)}, f32[8,1024]{1,0:T(8,128)}) custom-call(bf16[1024,1024]{1,0:T(8,128)(2,1)S(1)} %copy-done, bf16[1024,1024]{1,0:T(8,128)(2,1)} %bc_ref.1, f32[1024,1024]{1,0:T(8,128)} %get-tuple-element.7.gx0_ref, f32[1024,1024]{1,0:T(8,128)} %get-tuple-element.8.gbc0_ref, ...), custom_call_target="tpu_custom_call" | custom-call | tf_op jit(solution)/shard_map/carried_terms/pallas_call | solution.py:571
Async XLA Ops:
  0.6 128.5 %copy-start.1 = (f32[4,8,64,128]{3,2,1,0:T(8,128)S(1)}, f32[4,8,64,128]{3,2,1,0:T(8,128)}, u32[]{:S(2)}) copy-start(f32[4,8,64,128]{3,2,1,0:T(8,128)} %s_ref.1) | copy-start | bytes 3145732
  0.6 128.5 %copy-start.4 = (f32[8,1024]{1,0:T(8,128)S(1)}, f32[8,1024]{1,0:T(8,128)}, u32[]{:S(2)}) copy-start(f32[8,1024]{1,0:T(8,128)} %log_ref.3) | copy-start | bytes 98308
  0.7 128.5 %copy-start = (bf16[1024,1024]{1,0:T(8,128)(2,1)S(1)}, bf16[1024,1024]{1,0:T(8,128)(2,1)}, u32[]{:S(2)}) copy-start(bf16[1024,1024]{1,0:T(8,128)(2,1)} %x_ref.1) | copy-start | bytes 6291460
  129.2 1.2 copy-start.2
  130.4 0.9 copy-start.3

commit v3 on v2

--- a/solution.py
+++ b/solution.py
@@ -51,6 +51,7 @@
     bc_ref,
     far_w,
     acc,
+    mate_sum,
     sum_out,
     sum_in,
     weighted,
@@ -98,6 +99,7 @@
     has_left, has_right = z > 0, z < tp - 1
     inner = jnp.logical_and(has_left, has_right)
     outer = jnp.logical_not(inner)
+    low = jnp.where(z <= 1, 2, 0)
 
     def rows_of(c):
         return pl.ds(pl.multiple_of(c * CHUNK, CHUNK), CHUNK)
@@ -125,9 +127,19 @@
     def each(n, body):
         lax.fori_loop(0, n, lambda c, unused: (body(c), unused)[1], 0)
 
-    def term(s, c):
+    def rows_of_block(b):
+        return pl.ds(pl.multiple_of(b * BLOCK, BLOCK), BLOCK)
+
+    def term(s, rows):
         columns = pl.ds(pl.multiple_of(s * depth, depth), depth)
-        return lax.dot_general(got[s, rows_of(c)], w_ref[:, columns], LANES, preferred_element_type=F32)
+        return lax.dot_general(got[s, rows], w_ref[:, columns], LANES, preferred_element_type=F32)
+
+    def outward(s, rows):
+        columns = pl.ds(pl.multiple_of((s - low) * depth, depth), depth)
+        return lax.dot_general(got[s, rows], far_w[:, columns], LANES, preferred_element_type=F32)
+
+    def add_term(s, b):
+        acc[rows_of_block(b)] += term(s, rows_of_block(b))
 
     load_w = pltpu.make_async_copy(w_hbm, w_ref, local_sem.at[0])
     load_up = pltpu.make_async_copy(up_hbm, got.at[z], local_sem.at[1])
@@ -152,7 +164,6 @@
         pl.when(q != chip)(functools.partial(greet, ctx=2 * q + core))
     pl.semaphore_wait(barrier, chips + has_left.astype(jnp.int32) + has_right.astype(jnp.int32))
 
-    low = jnp.where(z <= 1, 2, 0)
 
     def piece_place(j):
         return far_w.at[pl.ds(pl.multiple_of(j * piece, piece), piece)]
@@ -187,10 +198,10 @@
     load_up.wait()
     load_w.wait()
 
-    def own_term(c):
-        acc[rows_of(c)] = term(z, c)
-
-    each(count, own_term)
+    def own_term(b):
+        acc[rows_of_block(b)] = term(z, rows_of_block(b))
+
+    each(blocks, own_term)
 
     if paired:
 
@@ -202,9 +213,6 @@
             piece_pair(chip).start()
 
     load_bc.wait()
-
-    def rows_of_block(b):
-        return pl.ds(pl.multiple_of(b * BLOCK, BLOCK), BLOCK)
 
     def weigh(b):
         here = rows_of_block(b)
@@ -263,13 +271,17 @@
         for copy in out_copies(b):
             copy.start()
 
-    def drain(arrive):
+    def drain(arrive, before=None, after=None):
         def take(b):
+            if before is not None:
+                before(b)
             for i in range(PER):
                 dy_ref[rows_of(b * PER + i)] = arrive(b, b * PER + i).astype(BF16)
                 pl.when(b > 0)(functools.partial(local_gradients, b - 1, i))
             pl.when(b > 0)(lambda: send_out(b - 1))
             block_terms(b)
+            if after is not None:
+                after(b)
 
         each(blocks, take)
 
@@ -292,26 +304,33 @@
                 pl.when(z == 2)(lambda: own_copy(c + count // 2, 0).start())
                 pl.when(z == 1)(lambda: own_copy(c + count // 2, 1).start())
 
-            acc[rows_of(c)] += term(end, c)
+        first_blocks = (blocks + 1) // 2
+
+        def first_block(b):
+            for i in range(PER):
+                first_hop(b * PER + i)
+            add_term(end, b)
+
+        def mate_block(b):
+            for i in range(PER):
+                relay(mate, b * PER + i, mate).wait_recv()
+            add_term(mate, b)
+            mate_sum[...] = outward(mate, rows_of_block(b))
 
         def second_hop(b, c):
-            early = c + count // 2
-            pl.when(early < count)(lambda: first_hop(early))
-            relay(mate, c, mate).wait_recv()
+            pl.when(b < blocks - first_blocks)(lambda: first_hop(c + first_blocks * PER))
             relay(far, c, mate).wait_recv()
-            outward = lax.dot_general(
-                got[low, rows_of(c)], far_w[:, :depth], LANES, preferred_element_type=F32
-            )
-            outward += lax.dot_general(
-                got[low + 1, rows_of(c)], far_w[:, depth:], LANES, preferred_element_type=F32
-            )
-            sum_out[rows_of(c)] = outward.astype(BF16)
+            in_block = pl.ds(pl.multiple_of((c - b * PER) * CHUNK, CHUNK), CHUNK)
+            sum_out[rows_of(c)] = (mate_sum[in_block] + outward(far, rows_of(c))).astype(BF16)
             sum_copy(c).start()
-            return acc[rows_of(c)] + term(mate, c) + term(far, c)
+            return acc[rows_of(c)] + term(far, rows_of(c))
+
+        def late_block(b):
+            pl.when(b < blocks - first_blocks)(lambda: add_term(end, b + first_blocks))
 
         @pl.when(inner)
         def _():
-            each(count // 2, first_hop)
+            each(first_blocks, first_block)
             for q in range(chips):
 
                 @pl.when(q != chip)
@@ -321,11 +340,12 @@
 
             for q in range(chips):
                 piece_wait(2 * q + 1 - core)
-            drain(second_hop)
-
-        def one_hop(c):
-            relay(next_in, c, next_in).wait_recv()
-            acc[rows_of(c)] += term(next_in, c)
+            drain(second_hop, mate_block, late_block)
+
+        def one_hop(b):
+            for i in range(PER):
+                relay(next_in, b * PER + i, next_in).wait_recv()
+            add_term(next_in, b)
 
         def last_sum(b, c):
             sum_copy(c).wait_recv()
@@ -333,7 +353,7 @@
 
         @pl.when(outer)
         def _():
-            each(count, one_hop)
+            each(blocks, one_hop)
             drain(last_sum)
 
     else:
@@ -344,13 +364,13 @@
                 def _():
                     relay(z - d, c, z + 1).wait_recv()
                     pl.when(has_right)(lambda: relay(z - d, c, z + 1).start())
-                    acc[rows_of(c)] += term(z - d, c)
+                    acc[rows_of(c)] += term(z - d, rows_of(c))
 
                 @pl.when(z + d < tp)
                 def _():
                     relay(z + d, c, z - 1).wait_recv()
                     pl.when(has_left)(lambda: relay(z + d, c, z - 1).start())
-                    acc[rows_of(c)] += term(z + d, c)
+                    acc[rows_of(c)] += term(z + d, rows_of(c))
 
             each(count, hop)
         drain(lambda b, c: acc[rows_of(c)])
@@ -475,6 +495,7 @@
             pltpu.VMEM(head_bc.shape, BF16),
             pltpu.VMEM((width, 2 * depth) if paired else (16, 128), BF16),
             pltpu.VMEM((tokens, width), F32),
+            pltpu.VMEM((BLOCK, width) if paired else (8, 128), F32),
             pltpu.VMEM(sums, BF16),
             pltpu.VMEM(sums, BF16),
             pltpu.VMEM((heads * STATE, tokens), BF16),
@@ -532,12 +553,11 @@
         here = slice(h * 128, (h + 1) * 128)
         bc = bc_ref[:, here]
         carried = h_ref[h]
-        held = carried.astype(BF16)
+        held = jnp.concatenate([carried, jnp.zeros_like(carried)], axis=0).astype(BF16)
         tail_h, whole_h = tail[:, h : h + 1], whole[:, h : h + 1]
-        added = jnp.dot(bc[:, :STATE], held, preferred_element_type=F32)
+        added = jnp.dot(bc, held, preferred_element_type=F32)
         gx_ref[:, here] = (gx0_ref[:, here] + tail_h * added).astype(BF16)
-        gb_tail = tail_h * lax.dot_general(x_ref[:, here], held, LANES, preferred_element_type=F32)
-        wide_tail = jnp.concatenate([gb_tail, jnp.zeros_like(gb_tail)], axis=1)
+        wide_tail = tail_h * lax.dot_general(x_ref[:, here], held, LANES, preferred_element_type=F32)
         gbc = gbc0_ref[:, here] + wide_tail
         gbc_ref[:, here] = gbc
         bc_wide = bc.astype(F32)
@@ -566,7 +586,7 @@
     block = pl.BlockSpec((1, heads, STATE, HEAD_DIM), lambda i: (blocks - 1 - i, 0, 0, 0))
     carry = pl.BlockSpec((heads, STATE, HEAD_DIM), lambda i: (0, 0, 0))
     params = pltpu.CompilerParams(
-        dimension_semantics=("arbitrary",), vmem_limit_bytes=48 * 1024 * 1024
+        dimension_semantics=("arbitrary",), vmem_limit_bytes=60 * 1024 * 1024
     )
     return pl.pallas_call(
         functools.partial(closing_kernel, heads),

time: 143 us -> 135 us (0.944)
  Pallas kernels: 140 us -> 134 us
  local copies, waits for them, and re-layouts: 2.18 us -> 0 us
    pallas_call x1, Pallas kernels: 128 us -> 121 us  [projected(): pl.pallas_call(functools.partial(project_kernel, tp, ctx), out_shape=(jax...]
    unnamed x10 -> x0, local copies, waits for them, and re-layouts: 2.18 us -> none
where the time goes in v3:
time: 135 us
  Pallas kernels  134 us (99%)
    pallas_call x1, Pallas kernels, projected(): pl.pallas_call(functools.partial(project_kernel, tp, ctx), out_shape=(jax...  121 us
    pallas_call x1, Pallas kernels, per_device(): pl.pallas_call(functools.partial(closing_kernel, heads), out_shape=(jax.S...  13.1 us

profile of v3, /device:TPU:0, one launch (start us, length us, event | category | flops | bytes accessed | tf_op | source)
XLA Modules:
  0.0 134.5 jit_solution(17953887473757579615)
XLA Ops:
  0.6 120.6 %project_and_exchange.1 = (f32[1024,1024]{1,0:T(8,128)}, f32[1024,1024]{1,0:T(8,128)}, f32[4,8,64,128]{3,2,1,0:T(8,128)}, f32[8,64,128]{2,1,0:T(8,128)}) custom-call(bf16[1024,1024]{1,0:T(8,128)(2,1)} %up_hbm.1, bf16[1024,4096]{1,0:T(8,128)(2,1)} %w_hbm.1, bf16[1024,1024]{1,0:T(8,128)(2,1)} %bc_ref.1, f32[8,1024]{1,0:T(8,128)} %log_ref.3, ...), custom_call_target="tpu_custom_call" | custom-call | tf_op jit(solution)/shard_map/project_and_exchange/pallas_call | solution.py:474
  121.3 13.1 %carried_terms.1 = (bf16[1024,1024]{1,0:T(8,128)(2,1)}, f32[1024,1024]{1,0:T(8,128)}, f32[8,1024]{1,0:T(8,128)}) custom-call(bf16[1024,1024]{1,0:T(8,128)(2,1)} %x_ref.1, bf16[1024,1024]{1,0:T(8,128)(2,1)} %bc_ref.1, f32[1024,1024]{1,0:T(8,128)} %get-tuple-element.7.gx0_ref, f32[1024,1024]{1,0:T(8,128)} %get-tuple-element.8.gbc0_ref, f32[8,1024]{1,0:T(8,128)} %log_ref.3, ...), custom_call_target="tpu_custom_call" | custom-call | tf_op jit(solution)/shard_map/carried_terms/pallas_call | solution.py:591

commit v4 on v3

--- a/solution.py
+++ b/solution.py
@@ -547,7 +547,7 @@
     whole, tail = jnp.exp(last), jnp.exp(last - cols)
     sign = jnp.where(lax.broadcasted_iota(jnp.int32, (1, 128), 1) < STATE, -1.0, 1.0)
     lane = lax.broadcasted_iota(jnp.int32, (BLOCK, heads), 1)
-    token = lax.broadcasted_iota(jnp.int32, (BLOCK, 1), 0)
+    at_end = []
     dcum = jnp.zeros((BLOCK, heads), F32)
     for h in range(heads):
         here = slice(h * 128, (h + 1) * 128)
@@ -562,16 +562,15 @@
         gbc_ref[:, here] = gbc
         bc_wide = bc.astype(F32)
         dcum_h = jnp.sum(bc_wide * gbc * sign, axis=1, keepdims=True)
-        at_end = whole_h * jnp.sum(s_ref[0, h] * carried) + jnp.sum(bc_wide * wide_tail)
-        dcum_h = dcum_h + jnp.where(token == BLOCK - 1, at_end, 0.0)
+        of_start = jnp.sum(s_ref[0, h] * carried, axis=0, keepdims=True)
+        at_end.append(whole_h * of_start + jnp.sum(bc_wide * wide_tail, axis=0, keepdims=True))
         dcum = jnp.where(lane == h, dcum_h, dcum)
         h_ref[h] = whole_h * carried + term_ref[0, h]
     s_ids = lax.broadcasted_iota(jnp.int32, (BLOCK, BLOCK), 0)
     t_ids = lax.broadcasted_iota(jnp.int32, (BLOCK, BLOCK), 1)
     from_here = jnp.where(s_ids >= t_ids, 1.0, 0.0)
-    glog_ref[...] = jnp.dot(
-        dcum.T, from_here, precision=lax.Precision.HIGHEST, preferred_element_type=F32
-    )
+    glog = jnp.dot(dcum.T, from_here, precision=lax.Precision.HIGHEST, preferred_element_type=F32)
+    glog_ref[...] = glog + jnp.sum(jnp.concatenate(at_end, axis=0), axis=1, keepdims=True)
 
 
 def per_device(upstream, out_weight, inner_act, head_bc, log_decay, states, skip):

time: 135 us -> 133 us (0.985)
  Pallas kernels: 134 us -> 132 us
    pallas_call x1, Pallas kernels: 13.1 us -> 11.3 us  [per_device(): pl.pallas_call(functools.partial(closing_kernel, heads), out_shape=(jax.S...]
where the time goes in v4:
time: 133 us
  Pallas kernels  132 us (99%)
    pallas_call x1, Pallas kernels, projected(): pl.pallas_call(functools.partial(project_kernel, tp, ctx), out_shape=(jax...  121 us
    pallas_call x1, Pallas kernels, per_device(): pl.pallas_call(functools.partial(closing_kernel, heads), out_shape=(jax.S...  11.3 us

profile of v4, /device:TPU:0, one launch (start us, length us, event | category | flops | bytes accessed | tf_op | source)
XLA Modules:
  0.0 132.6 jit_solution(1181160592867673558)
XLA Ops:
  0.6 120.6 %project_and_exchange.1 = (f32[1024,1024]{1,0:T(8,128)}, f32[1024,1024]{1,0:T(8,128)}, f32[4,8,64,128]{3,2,1,0:T(8,128)}, f32[8,64,128]{2,1,0:T(8,128)}) custom-call(bf16[1024,1024]{1,0:T(8,128)(2,1)} %up_hbm.1, bf16[1024,4096]{1,0:T(8,128)(2,1)} %w_hbm.1, bf16[1024,1024]{1,0:T(8,128)(2,1)} %bc_ref.1, f32[8,1024]{1,0:T(8,128)} %log_ref.3, ...), custom_call_target="tpu_custom_call" | custom-call | tf_op jit(solution)/shard_map/project_and_exchange/pallas_call | solution.py:474
  121.3 11.3 %carried_terms.1 = (bf16[1024,1024]{1,0:T(8,128)(2,1)}, f32[1024,1024]{1,0:T(8,128)}, f32[8,1024]{1,0:T(8,128)}) custom-call(bf16[1024,1024]{1,0:T(8,128)(2,1)} %x_ref.1, bf16[1024,1024]{1,0:T(8,128)(2,1)} %bc_ref.1, f32[1024,1024]{1,0:T(8,128)} %get-tuple-element.7.gx0_ref, f32[1024,1024]{1,0:T(8,128)} %get-tuple-element.8.gbc0_ref, f32[8,1024]{1,0:T(8,128)} %log_ref.3, ...), custom_call_target="tpu_custom_call" | custom-call | tf_op jit(solution)/shard_map/carried_terms/pallas_call | solution.py:590
